TPU v7x, 128 devices: a whole 4x4x4 slice. The times are simulated.
128 devices in a mesh: seq: 16 (over x, y), section: 8 (over z, core).
Axes of the slice: x: 4, y: 4, z: 4, core: 2. Of those that a mesh axis runs over, the one named last changes fastest.
Arguments:
- hidden: bfloat16 [8, 6144, 2560], P('section', 'seq'), may hold values from -6 to 6
- query_norm_gain: float32 [8, 2560], P('section'), may hold values from 0.25 to 1.75
- key_norm_gain: float32 [8, 2560], P('section'), may hold values from 0.25 to 1.75
- text_kv: bfloat16 [8, 16, 2, 512, 2560], P('section', 'seq'), may hold values from -6 to 6
- holder: int32 [8], P('section'), may hold values from 0 to 15
- pattern: int32 [48, 7], replicated, may hold values from 0 to 1, as said below
- grad_out: bfloat16 [8, 6144, 2560], P('section', 'seq'), may hold values from -6 to 6
Outputs:
- attended: bfloat16 [8, 6144, 2560], P('section', 'seq')
- upstream: bfloat16 [8, 6144, 2560], P('section', 'seq')
- text_grad: bfloat16 [8, 2, 512, 2560], P('section')
Inputs may be any that keep to these rules, and one draw needn't show every extreme that they name: pattern[b, 3] = 1 for every block b; entries are 0 or 1.
All inputs are finite; a program needn't handle non-finite values.
Results may differ from a plain program's by a relative error of at most 0.0078.
Values may be sent and summed in bfloat16 or wider, within the bound.
A program may use at most 256 MiB of HBM per device.

v0:
```python
import jax
import jax.numpy as jnp
from jax import lax
from jax.sharding import PartitionSpec as P

HDIM = 128
BLK = 128
eps = 1e-06


def extended(cells, sides, width):
    for axis, dim in sides:
        count = lax.axis_size(axis)
        ends = count - 1
        head = lax.slice_in_dim(cells, 0, width, axis=dim)
        tail = lax.slice_in_dim(cells, cells.shape[dim] - width, cells.shape[dim], axis=dim)
        cells = jnp.concatenate(
            [
                lax.ppermute(tail, axis, [(i, (i + 1) % count) for i in range(ends)]),
                cells,
                lax.ppermute(head, axis, [((i + 1) % count, i) for i in range(ends)]),
            ],
            axis=dim,
        )
    return cells


def from_root(block, axis, owner):
    block = jnp.where(lax.axis_index(axis) == owner, block, jnp.zeros_like(block))
    return lax.psum(block, axis)


def shifted(x, axis, by):
    peers = lax.axis_size(axis)
    pairs = [(i, i + by) for i in range(peers) if 0 <= i + by < peers]
    return lax.ppermute(x, axis, pairs)


def norm_forward(hidden_state, norm_gain):
    hidden_float = hidden_state.astype(jnp.float32)
    inverse_root_norm = lax.rsqrt(
        jnp.mean(hidden_float * hidden_float, axis=-1, keepdims=True) + eps
    )
    normalized_input = hidden_float * inverse_root_norm
    return (
        (normalized_input * norm_gain).astype(jnp.bfloat16),
        normalized_input,
        inverse_root_norm,
    )


def norm_backward(upper_bound, norm_gain, normalized_input, inverse_root_norm):
    scaled_input = upper_bound * norm_gain
    return inverse_root_norm * (
        scaled_input
        - normalized_input * jnp.mean(scaled_input * normalized_input, axis=-1, keepdims=True)
    )


def block_mask(pattern, slab, bpd, nslab):
    span = pattern.shape[1]
    rows = lax.dynamic_slice_in_dim(pattern, slab * bpd, bpd, 0)
    first = jnp.arange(bpd, dtype=jnp.int32)[:, None]
    second = jnp.arange(3 * bpd, dtype=jnp.int32)[None, :]
    offset = second - first
    onehot = offset[:, :, None] == jnp.arange(span, dtype=jnp.int32)[None, None, :]
    picked = jnp.sum(jnp.where(onehot, rows[:, None, :], 0), axis=-1)
    globe = slab * bpd - bpd + second
    inside = (globe >= 0) & (globe < nslab * bpd)
    return (picked > 0) & inside


def token_mask(blocks):
    return jnp.repeat(jnp.repeat(blocks, BLK, axis=0), BLK, axis=1)


def divide_heads(x):
    return x.reshape(x.shape[0], x.shape[1] // HDIM, HDIM).transpose(1, 0, 2)


def join_heads(x):
    return x.transpose(1, 0, 2).reshape(x.shape[1], x.shape[0] * x.shape[2])


def query_side(qh, kh, vh, tkh, tvh, doh, attend_mask):
    scale = qh.shape[-1] ** (-0.5)
    keys = jnp.concatenate([kh, tkh], axis=0)
    vals = jnp.concatenate([vh, tvh], axis=0)
    full = jnp.concatenate([attend_mask, jnp.ones((qh.shape[0], tkh.shape[0]), bool)], axis=1)
    scores = jnp.dot(qh, keys.T, preferred_element_type=jnp.float32) * scale
    scores = jnp.where(full, scores, -1e30)
    top = jnp.max(scores, axis=1, keepdims=True)
    total = jnp.sum(jnp.where(full, jnp.exp(scores - top), 0.0), axis=1, keepdims=True)
    lse = top + jnp.log(total)
    probs = jnp.where(full, jnp.exp(scores - lse), 0.0)
    probs_b = probs.astype(jnp.bfloat16)
    out = jnp.dot(probs_b, vals, preferred_element_type=jnp.float32)
    dprob = jnp.dot(doh, vals.T, preferred_element_type=jnp.float32)
    delta = jnp.sum(doh.astype(jnp.float32) * out, axis=1)
    dscore = (probs * (dprob - delta[:, None]) * scale).astype(jnp.bfloat16)
    query_gradient = jnp.dot(dscore, keys, preferred_element_type=jnp.float32)
    dkeys = jnp.dot(dscore.T, qh, preferred_element_type=jnp.float32)
    dvals = jnp.dot(probs_b.T, doh, preferred_element_type=jnp.float32)
    return (out, lse[:, 0], delta, query_gradient, dkeys, dvals)


def local(hidden, query_norm_gain, key_norm_gain, text_kv, holder, pattern, grad_out):
    hidden_state = hidden[0]
    output_gradient = grad_out[0]
    token_rows = hidden_state.shape[0]
    bpd = token_rows // BLK
    slab = lax.axis_index("seq")
    nslab = lax.axis_size("seq")
    normed_query, normalized_input, inverse_root_norm = norm_forward(
        hidden_state, query_norm_gain[0]
    )
    kn, _, _ = norm_forward(hidden_state, key_norm_gain[0])
    near = extended(jnp.stack([kn, hidden_state]), (("seq", 1),), token_rows)
    text_tokens = from_root(text_kv[0, 0], "seq", holder[0])
    attend_mask = token_mask(block_mask(pattern, slab, bpd, nslab))

    def each_head_value(a):
        return query_side(a[0], a[1], a[2], a[3], a[4], a[5], attend_mask)

    saved_residuals = lax.map(
        each_head_value,
        (
            divide_heads(normed_query),
            divide_heads(near[0]),
            divide_heads(near[1]),
            divide_heads(text_tokens[0]),
            divide_heads(text_tokens[1]),
            divide_heads(output_gradient),
        ),
    )
    out, lse, delta, query_gradient, dkeys, dvals = saved_residuals
    ext_rows = 3 * token_rows
    dtext_part = jnp.stack([join_heads(dkeys[:, ext_rows:]), join_heads(dvals[:, ext_rows:])])
    ext = jnp.stack([join_heads(dkeys[:, :ext_rows]), join_heads(dvals[:, :ext_rows])])
    from_upper = shifted(ext[:, :token_rows].astype(jnp.bfloat16), "seq", -1).astype(jnp.float32)
    from_lower = shifted(ext[:, 2 * token_rows :].astype(jnp.bfloat16), "seq", 1).astype(
        jnp.float32
    )
    own_rows = ext[:, token_rows : 2 * token_rows] + from_upper + from_lower
    text_total = lax.psum(dtext_part, "seq")
    grad_hidden = (
        own_rows[1]
        + norm_backward(
            join_heads(query_gradient), query_norm_gain[0], normalized_input, inverse_root_norm
        )
        + norm_backward(own_rows[0], key_norm_gain[0], normalized_input, inverse_root_norm)
    )
    upstream = shifted(grad_hidden.astype(jnp.bfloat16), "section", -1)
    attended = join_heads(out).astype(jnp.bfloat16)
    return (attended[None], upstream[None], text_total.astype(jnp.bfloat16)[None])


def solution(mesh):
    in_specs = (
        P("section", "seq", None),
        P("section", None),
        P("section", None),
        P("section", "seq", None, None, None),
        P("section"),
        P(),
        P("section", "seq", None),
    )
    out_specs = (
        P("section", "seq", None),
        P("section", "seq", None),
        P("section", None, None, None),
    )
    return jax.shard_map(local, mesh=mesh, in_specs=in_specs, out_specs=out_specs, check_vma=False)
```

profile of v0, /device:TPU:24, one launch (start us, length us, event | category | flops | bytes accessed | tf_op | source)
XLA Modules:
  0.0 923.3 jit_solution(16334344849139469414)
XLA Ops:
  7.2 2.8 copy.43
  12.4 2.3 pad_maximum_fusion.9
  14.7 2.6 collective-permute-start.1
  17.4 5.3 collective-permute-start
  23.4 8.0 copy.45
  31.3 2.7 select_bitcast_fusion
  34.7 4.0 copy.46
  38.7 3.2 fusion.42
  41.9 93.5 %collective-permute-done.1 = bf16[2,384,2560]{1,2,0:T(8,128)(2,1)} collective-permute-done((bf16[2,384,2560]{1,2,0:T(8,128)(2,1)}, bf16[2,384,2560]{1,2,0:T(8,128)(2,1)}, u32[]{:S(2)}, u32[]{:S(2)}) %collective-permute-start.1) | collective-permute-done | bytes 3932192 | tf_op jit(solution)/shard_map/ppermute | solution.py:21
  135.4 3.1 collective-permute-done
  138.5 5.1 pad_maximum_fusion.7
  143.7 4.9 fusion.45
  148.6 26.1 %all-reduce.4.cloned.1.call-done = bf16[2,512,2560]{1,2,0:T(8,128)(2,1)} async-done(((bf16[2,512,2560]{1,2,0:T(8,128)(2,1)}), bf16[2,512,2560]{1,2,0:T(8,128)(2,1)}) %all-reduce.4.cloned.1.call-update) | async-done | bytes 5242896 | tf_op jit(solution)/shard_map/psum | solution.py:30
  174.6 5.2 fusion.46
  179.8 351.3 %while.17 = (s32[]{:T(128)}, bf16[20,384,128]{1,2,0:T(8,128)(2,1)}, f32[20,384,128]{1,2,0:T(8,128)}, f32[20,1664,128]{1,2,0:T(8,128)}, f32[20,1664,128]{1,2,0:T(...) while((s32[]{:T(128)}, bf16[20,384,128]{1,2,0:T(8,128)(2,1)}, ...), condition=%wide.region_7.8_spmd.clone, body=%wide.region_3.7_spmd.clone.sunk | while | flops 996523264 | bytes 28792892 | solution.py:125
  192.6 2.5 fusion.70
  203.8 2.3 bitcast_dynamic-update-slice_fusion.2
  210.1 2.6 fusion.70
  227.7 2.5 fusion.70
  238.8 2.3 bitcast_dynamic-update-slice_fusion.2
  245.2 2.6 fusion.70
  262.8 2.5 fusion.70
  273.9 2.3 bitcast_dynamic-update-slice_fusion.2
  280.3 2.5 fusion.70
  291.4 2.3 bitcast_dynamic-update-slice_fusion.2
  297.8 2.6 fusion.70
  309.0 2.3 bitcast_dynamic-update-slice_fusion.2
  315.4 2.5 fusion.70
  326.6 2.3 bitcast_dynamic-update-slice_fusion.2
  332.9 2.6 fusion.70
  344.1 2.3 bitcast_dynamic-update-slice_fusion.2
  350.5 2.6 fusion.70
  368.1 2.6 fusion.70
  379.5 2.3 bitcast_dynamic-update-slice_fusion.2
  385.8 2.5 fusion.70
  397.0 2.3 bitcast_dynamic-update-slice_fusion.2
  403.4 2.5 fusion.70
  414.5 2.3 bitcast_dynamic-update-slice_fusion.2
  420.9 2.5 fusion.70
  432.0 2.3 bitcast_dynamic-update-slice_fusion.2
  438.4 2.6 fusion.70
  449.6 2.3 bitcast_dynamic-update-slice_fusion.2
  456.0 2.6 fusion.70
  473.6 2.5 fusion.70
  491.2 2.5 fusion.70
  508.7 2.6 fusion.70
  526.3 2.6 fusion.70
  531.1 9.7 %slice.46 = f32[20,1152,128]{1,2,0:T(8,128)} slice(f32[20,1664,128]{1,2,0:T(8,128)} %get-tuple-element.70), slice={[0:20], [0:1152], [0:128]} | slice | bytes 23592960 | tf_op jit(solution)/shard_map/slice | solution.py:139
  540.9 9.7 %slice.45 = f32[20,1152,128]{1,2,0:T(8,128)} slice(f32[20,1664,128]{1,2,0:T(8,128)} %get-tuple-element.69), slice={[0:20], [0:1152], [0:128]} | slice | bytes 23592960 | tf_op jit(solution)/shard_map/slice | solution.py:139
  550.6 9.0 fusion.29
  559.6 3.6 fusion.44
  563.2 2.7 collective-permute-start.2
  565.9 5.4 collective-permute-start.3
  571.3 5.7 slice.53
  577.0 5.6 slice.52
  582.6 10.1 %pad_maximum_fusion.8 = f32[2,512,2560]{1,2,0:T(8,128)} fusion(f32[1,512,2560]{1,2,0:T(8,128)} %bitcast.170, f32[1,512,2560]{1,2,0:T(8,128)} %bitcast.171), kind=kLoop, calls=%fused_computation.47 | loop fusion | flops 2621440 | bytes 20971520 | tf_op jit(solution)/shard_map/stack | solution.py:138
  592.7 3.9 fusion.40
  596.7 57.5 %collective-permute-done.2 = bf16[2,384,2560]{1,2,0:T(8,128)(2,1)} collective-permute-done((bf16[2,384,2560]{1,2,0:T(8,128)(2,1)}, bf16[2,384,2560]{1,2,0:T(8,128)(2,1)}, u32[]{:S(2)}, u32[]{:S(2)}) %collective-permute-start.2) | collective-permute-done | bytes 3932192 | tf_op jit(solution)/shard_map/ppermute | solution.py:36
  655.4 5.0 fusion.32
  662.5 3.0 fusion.36
  666.9 235.2 %all-reduce.5 = bf16[2,512,2560]{1,2,0:T(8,128)(2,1)} all-reduce(f32[2,512,2560]{1,2,0:T(8,128)} %pad_maximum_fusion.8), channel_id=1, replica_groups=mesh['seq'=16,'section'=8] {'seq'}, use_global_device_ids=true, to_apply=%region_10.11 | all-reduce | flops 2621440 | bytes 15728640 | tf_op jit(solution)/shard_map/psum | solution.py:145
  902.2 2.4 copy.60
  904.6 7.9 copy.62
  912.5 4.0 copy.61
  (398 shorter events, 279.3 us)
Async XLA Ops:
  7.2 26.9 %copy-start = (s32[48,7]{0,1:T(8,128)S(1)}, s32[48,7]{0,1:T(8,128)}, u32[]{:S(2)}) copy-start(s32[48,7]{0,1:T(8,128)} %param.14) | copy-start | bytes 4036
  7.2 3.4 copy-start.7
  7.2 167.4 %all-reduce.4.cloned.1.call-start = ((), (), s32[]{:S(2)}) async-start(), calls=%async_computation | async-start | bytes 10485760 | tf_op jit(solution)/shard_map/psum | solution.py:30
  11.1 1.3 copy-start.2
  14.7 120.7 %collective-permute-start.1 = (bf16[2,384,2560]{1,2,0:T(8,128)(2,1)}, bf16[2,384,2560]{1,2,0:T(8,128)(2,1)}, u32[]{:S(2)}, u32[]{:S(2)}) collective-permute-start(bf16[2,384,2560]{1,2,0:T(8,128)(2,1)} %pad_maximum_fusion.9), channel_id=1, source_target_pairs={{8,0},{16,8},{24,16},{32,24},{40,32},{48,40},{56,48},{64,56},{72,6... | collective-permute-start | bytes 11796488 | tf_op jit(solution)/shard_map/ppermute | solution.py:21
  17.4 121.1 %collective-permute-start = (bf16[2,384,2560]{1,2,0:T(8,128)(2,1)}, bf16[2,384,2560]{1,2,0:T(8,128)(2,1)}, u32[]{:S(2)}, u32[]{:S(2)}) collective-permute-start(bf16[2,384,2560]{1,2,0:T(8,128)(2,1)} %pad_maximum_fusion.9), channel_id=1, source_target_pairs={{0,8},{8,16},{16,24},{24,32},{32,40},{40,48},{48,56},{56,64},{64,7... | collective-permute-start | bytes 11796488 | tf_op jit(solution)/shard_map/ppermute | solution.py:19
  34.0 0.7 copy-start.8
  38.7 99.8 %copy-start.3 = (bf16[1,384,2560]{1,2,0:T(8,128)(2,1)S(1)}, bf16[1,384,2560]{1,2,0:T(8,128)(2,1)}, u32[]{:S(2)}) copy-start(bf16[1,384,2560]{1,2,0:T(8,128)(2,1)} %copy-done.2) | copy-start | bytes 5898244
  185.6 3.9 copy-start.5
  203.1 3.9 copy-start.5
  220.7 3.9 copy-start.5
  238.2 3.9 copy-start.5
  255.7 3.9 copy-start.5
  273.3 3.9 copy-start.5
  290.8 3.9 copy-start.5
  308.3 3.9 copy-start.5
  325.9 3.9 copy-start.5
  343.4 3.9 copy-start.5
  361.1 3.9 copy-start.5
  378.8 3.9 copy-start.5
  396.3 3.9 copy-start.5
  413.8 3.9 copy-start.5
  431.4 3.9 copy-start.5
  448.9 3.9 copy-start.5
  466.6 3.9 copy-start.5
  484.1 3.9 copy-start.5
  501.7 3.9 copy-start.5
  519.3 3.9 copy-start.5
  563.2 91.0 %collective-permute-start.2 = (bf16[2,384,2560]{1,2,0:T(8,128)(2,1)}, bf16[2,384,2560]{1,2,0:T(8,128)(2,1)}, u32[]{:S(2)}, u32[]{:S(2)}) collective-permute-start(bf16[2,384,2560]{1,2,0:T(8,128)(2,1)} %get-tuple-element.175), channel_id=1, source_target_pairs={{8,0},{16,8},{24,16},{32,24},{40,32},{48,40},{56,48},{64,56},{72,6... | collective-permute-start | bytes 11796488 | tf_op jit(solution)/shard_map/ppermute | solution.py:36
  565.9 89.4 %collective-permute-start.3 = (bf16[2,384,2560]{1,2,0:T(8,128)(2,1)}, bf16[2,384,2560]{1,2,0:T(8,128)(2,1)}, u32[]{:S(2)}, u32[]{:S(2)}) collective-permute-start(bf16[2,384,2560]{1,2,0:T(8,128)(2,1)} %get-tuple-element.176), channel_id=1, source_target_pairs={{0,8},{8,16},{16,24},{24,32},{32,40},{40,48},{48,56},{56,64},{64,7... | collective-permute-start | bytes 11796488 | tf_op jit(solution)/shard_map/ppermute | solution.py:36
  582.6 72.8 %slice-start = ((s8[11796480]{0:T(1024)(128)(4,1)}), s8[4194304]{0:T(1024)(128)(4,1)S(1)}, s32[]{:S(2)}) async-start(s8[11796480]{0:T(1024)(128)(4,1)} %bitcast.162), calls=%async_computation.1 | async-start | bytes 8388608
  582.6 72.8 %slice-start.1 = ((s8[11796480]{0:T(1024)(128)(4,1)}), s8[4194304]{0:T(1024)(128)(4,1)S(1)}, s32[]{:S(2)}) async-start(s8[11796480]{0:T(1024)(128)(4,1)} %bitcast.162), calls=%async_computation.2 | async-start | bytes 8388608
  582.6 72.8 %slice-start.2 = ((s8[11796480]{0:T(1024)(128)(4,1)}), s8[3407872]{0:T(1024)(128)(4,1)S(1)}, s32[]{:S(2)}) async-start(s8[11796480]{0:T(1024)(128)(4,1)} %bitcast.162), calls=%async_computation.3 | async-start | bytes 6815744
  660.4 2.1 copy-start.4
  665.5 236.7 %copy-start.6 = (bf16[20,384,128]{1,2,0:T(8,128)(2,1)S(1)}, bf16[20,384,128]{1,2,0:T(8,128)(2,1)}, u32[]{:S(2)}) copy-start(bf16[20,384,128]{1,2,0:T(8,128)(2,1)} %get-tuple-element.68) | copy-start | bytes 5898244
  665.5 247.0 %collective-permute-start.4 = (bf16[384,2560]{0,1:T(8,128)(2,1)}, bf16[384,2560]{0,1:T(8,128)(2,1)}, u32[]{:S(2)}, u32[]{:S(2)}) collective-permute-start(bf16[384,2560]{0,1:T(8,128)(2,1)} %fusion.36), channel_id=1, source_target_pairs={{1,0},{2,1},{3,2},{4,3},{5,4},{6,5},{7,6},{9,8},{10,9},{11,10},{12... | collective-permute-start | bytes 5898248 | tf_op jit(solution)/shard_map/ppermute | solution.py:36
  904.6 11.9 %copy-start.1 = (s32[48,7]{0,1:T(8,128)S(1)}, s32[48,7]{0,1:T(8,128)}, u32[]{:S(2)}) copy-start(s32[48,7]{0,1:T(8,128)} %param.14) | copy-start | bytes 4036
Sparse Core Ops, SparseCore 0:
  34.2 140.4 all-reduce.3
where the time goes:
time: 929 us; the launch traced here: 923 us
  matrix products  237 us (26%)
  blocking collectives  235 us (25%)
  waiting for transfers between devices  181 us (19%)
  local copies, waits for them, and re-layouts  158 us (17%)
  other arithmetic  78.9 us (8%)
  starting transfers between devices  17.5 us (2%)
  between operations  14.9 us (2%)
    psum x1, blocking collectives, local(): text_total = lax.psum(dtext_part, 'seq')  235 us
    ppermute x1, waiting for transfers between devices, extended(): lax.ppermute(head, axis, [((i + 1) % count, i) for i in range(ends)])  93.5 us
    dynamic_slice x120, local copies, waits for them, and re-layouts, local(): lax.map(each_head_value, (divide_heads(normed_query), divide_heads(near[0...  68.1 us
    ppermute x3, waiting for transfers between devices, shifted(): return lax.ppermute(x, axis, pairs)  58.7 us
    dot_general x20, matrix products, query_side(): dvals = jnp.dot(probs_b.T, doh, preferred_element_type=jnp.float32)  51.2 us
    dot_general x20, matrix products, query_side(): out = jnp.dot(probs_b, vals, preferred_element_type=jnp.float32)  46 us
    dot_general x20, matrix products, query_side(): dkeys = jnp.dot(dscore.T, qh, preferred_element_type=jnp.float32)  44.5 us
    dot_general x20, matrix products, query_side(): dprob = jnp.dot(doh, vals.T, preferred_element_type=jnp.float32)  38.1 us
  transfers between devices with their start and end apart: 6, of which 5 were waited for; matrix products, arithmetic and copies ran while one was open for 7% of the time, Pallas kernels for 0%

commit v1 on v0

--- a/solution.py
+++ b/solution.py
@@ -142,7 +142,7 @@
         jnp.float32
     )
     own_rows = ext[:, token_rows : 2 * token_rows] + from_upper + from_lower
-    text_total = lax.psum(dtext_part, "seq")
+    text_total = jnp.sum(lax.all_gather(dtext_part, "seq"), axis=0)
     grad_hidden = (
         own_rows[1]
         + norm_backward(

time: 929 us -> 1570 us (1.69)
  waiting for transfers between devices: 181 us -> 1010 us
  blocking collectives: 235 us -> 0 us
  other arithmetic: 78.9 us -> 132 us
  matrix products: 237 us -> 218 us
    all_gather x0 -> x1, waiting for transfers between devices: none -> 718 us  [local(): text_total = jnp.sum(lax.all_gather(dtext_part, 'seq'), axis=0)]
    psum x1 -> x0, blocking collectives: 235 us -> none  [local(): text_total = lax.psum(dtext_part, 'seq')]
    ppermute x3, waiting for transfers between devices: 58.7 us -> 174 us  [shifted(): return lax.ppermute(x, axis, pairs)]
    reduce_sum x0 -> x1, other arithmetic: none -> 54.1 us  [local(): text_total = jnp.sum(lax.all_gather(dtext_part, 'seq'), axis=0)]
    dot_general x20, matrix products: 46 us -> 27.8 us  [query_side(): out = jnp.dot(probs_b, vals, preferred_element_type=jnp.float32)]
    unnamed x31 -> x40, local copies, waits for them, and re-layouts: 31.5 us -> 38.2 us
  transfers between devices with their start and end apart: 6 -> 7, of which waited for: 5 -> 7; matrix products, arithmetic and copies ran while one was open for 7% -> 6% of each run, Pallas kernels for 0% -> 0%
where the time goes in v1:
time: 1570 us; the launch traced here: 1560 us
  waiting for transfers between devices  1010 us (64%)
  matrix products  218 us (14%)
  local copies, waits for them, and re-layouts  169 us (11%)
  other arithmetic  132 us (8%)
    all_gather x1, waiting for transfers between devices, local(): text_total = jnp.sum(lax.all_gather(dtext_part, 'seq'), axis=0)  718 us
    ppermute x3, waiting for transfers between devices, shifted(): return lax.ppermute(x, axis, pairs)  174 us
    ppermute x1, waiting for transfers between devices, extended(): lax.ppermute(head, axis, [((i + 1) % count, i) for i in range(ends)])  93.2 us
    dynamic_slice x120, local copies, waits for them, and re-layouts, local(): lax.map(each_head_value, (divide_heads(normed_query), divide_heads(near[0...  55.5 us
    reduce_sum x1, other arithmetic, local(): text_total = jnp.sum(lax.all_gather(dtext_part, 'seq'), axis=0)  54.1 us
    dot_general x20, matrix products, query_side(): dvals = jnp.dot(probs_b.T, doh, preferred_element_type=jnp.float32)  51.1 us
    dot_general x20, matrix products, query_side(): dkeys = jnp.dot(dscore.T, qh, preferred_element_type=jnp.float32)  44.3 us
    unnamed x40, local copies, waits for them, and re-layouts  38.2 us
  transfers between devices with their start and end apart: 7, of which 7 were waited for; matrix products, arithmetic and copies ran while one was open for 6% of the time, Pallas kernels for 0%

profile of v1, /device:TPU:24, one launch (start us, length us, event | category | flops | bytes accessed | tf_op | source)
XLA Modules:
  0.0 1564.3 jit_solution(17958936751596153889)
XLA Ops:
  7.2 2.8 copy.62
  11.2 2.6 pad_maximum_fusion.9
  13.7 2.6 collective-permute-start.1
  16.4 5.3 collective-permute-start
  21.7 8.0 copy.64
  30.3 2.7 select_bitcast_fusion
  33.8 4.0 copy.65
  38.0 3.2 fusion.42
  41.2 93.2 %collective-permute-done.1 = bf16[2,384,2560]{1,2,0:T(8,128)(2,1)} collective-permute-done((bf16[2,384,2560]{1,2,0:T(8,128)(2,1)}, bf16[2,384,2560]{1,2,0:T(8,128)(2,1)}, u32[]{:S(2)}, u32[]{:S(2)}) %collective-permute-start.1) | collective-permute-done | bytes 3932192 | tf_op jit(solution)/shard_map/ppermute | solution.py:21
  134.4 3.1 collective-permute-done
  137.5 5.1 pad_maximum_fusion.7
  142.7 4.9 fusion.45
  147.5 26.1 %all-reduce.3.cloned.1.call-done = bf16[2,512,2560]{1,2,0:T(8,128)(2,1)} async-done(((bf16[2,512,2560]{1,2,0:T(8,128)(2,1)}), bf16[2,512,2560]{1,2,0:T(8,128)(2,1)}) %all-reduce.3.cloned.1.call-update) | async-done | bytes 5242896 | tf_op jit(solution)/shard_map/psum | solution.py:30
  173.6 5.2 fusion.46
  178.9 319.6 %while.17 = (s32[]{:T(128)}, bf16[20,384,128]{1,2,0:T(8,128)(2,1)}, f32[20,384,128]{1,2,0:T(8,128)}, f32[20,1664,128]{1,2,0:T(8,128)}, f32[20,1664,128]{1,2,0:T(...) while((s32[]{:T(128)}, bf16[20,384,128]{1,2,0:T(8,128)(2,1)}, ...), condition=%wide.region_7.8_spmd.clone, body=%wide.region_3.7_spmd.clone.sunk | while | flops 996523264 | bytes 28268576 | solution.py:125
  192.3 2.6 fusion.70
  206.1 2.2 fusion.69
  208.3 2.6 fusion.70
  224.3 2.5 fusion.70
  240.2 2.5 fusion.70
  253.9 2.2 fusion.69
  256.2 2.5 fusion.70
  270.0 2.2 fusion.69
  272.2 2.6 fusion.70
  288.1 2.5 fusion.70
  301.9 2.2 fusion.69
  304.1 2.6 fusion.70
  320.1 2.5 fusion.70
  333.8 2.2 fusion.69
  336.1 2.6 fusion.70
  352.1 2.6 fusion.70
  365.8 2.2 fusion.69
  368.1 2.6 fusion.70
  384.1 2.6 fusion.70
  400.0 2.6 fusion.70
  416.0 2.6 fusion.70
  429.8 2.2 fusion.69
  432.0 2.6 fusion.70
  445.8 2.2 fusion.69
  448.0 2.6 fusion.70
  461.8 2.2 fusion.69
  464.0 2.6 fusion.70
  480.0 2.6 fusion.70
  496.0 2.5 fusion.70
  498.5 3.3 slice.53
  501.9 3.3 slice.52
  505.2 5.2 pad_maximum_fusion.8
  510.4 11.4 copy.79
  521.9 10.3 slice.45
  532.2 16.1 %slice.46 = f32[20,1152,128]{1,2,0:T(8,128)} slice(f32[20,1664,128]{1,2,0:T(8,128)} %get-tuple-element.70), slice={[0:20], [0:1152], [0:128]} | slice | bytes 23592960 | tf_op jit(solution)/shard_map/slice | solution.py:139
  548.3 17.4 %fusion.29 = bf16[2,1152,2560]{1,2,0:T(8,128)(2,1)} fusion(f32[1,1152,2560]{1,2,0:T(8,128)} %bitcast.166, f32[1,1152,2560]{1,2,0:T(8,128)} %bitcast.162), kind=kLoop, calls=%fused_computation.45 | loop fusion | flops 5898240 | bytes 35389440 | tf_op jit(solution)/shard_map/convert.3
  565.7 6.8 fusion.44
  572.5 3.9 collective-permute-start.3
  576.4 2.3 collective-permute-start.2
  579.4 167.3 %collective-permute-done.3 = bf16[2,384,2560]{1,2,0:T(8,128)(2,1)} collective-permute-done((bf16[2,384,2560]{1,2,0:T(8,128)(2,1)}, bf16[2,384,2560]{1,2,0:T(8,128)(2,1)}, u32[]{:S(2)}, u32[]{:S(2)}) %collective-permute-start.3) | collective-permute-done | bytes 3932192 | tf_op jit(solution)/shard_map/ppermute | solution.py:36
  746.8 5.6 collective-permute-done.2
  752.4 4.0 fusion.32
  758.5 3.0 fusion.36
  762.8 4.0 copy.81
  767.6 2.4 copy.82
  770.0 717.5 %all-gather.3.cloned.1.call-done = f32[32,512,2560]{2,1,0:T(8,128)} async-done(((f32[2,512,2560]{2,1,0:T(8,128)}), f32[32,512,2560]{2,1,0:T(8,128)}) %all-gather.3.cloned.1.call-update) | async-done | bytes 167772176 | tf_op jit(solution)/shard_map/all_gather | solution.py:145
  1487.5 54.1 %reduce_sum.71 = bf16[2,512,2560]{2,1,0:T(8,128)(2,1)} reduce(f32[16,2,512,2560]{3,2,1,0:T(8,128)} %bitcast.30, f32[]{:T(128)} %constant.36.clone.1), dimensions={0}, to_apply=%region_10.11 | reduce | flops 39321600 | bytes 173015040 | tf_op jit(solution)/shard_map/reduce_sum | solution.py:145
  1541.6 7.9 copy.95
  1549.5 7.9 copy.83
  (372 shorter events, 254.5 us)
Async XLA Ops:
  7.2 26.1 %copy-start = (s32[48,7]{0,1:T(8,128)S(1)}, s32[48,7]{0,1:T(8,128)}, u32[]{:S(2)}) copy-start(s32[48,7]{0,1:T(8,128)} %param.14) | copy-start | bytes 4036
  7.2 3.4 copy-start.7
  7.2 166.5 %all-reduce.3.cloned.1.call-start = ((), (), s32[]{:S(2)}) async-start(), calls=%async_computation | async-start | bytes 10485760 | tf_op jit(solution)/shard_map/psum | solution.py:30
  11.1 2.6 copy-start.2
  13.7 120.7 %collective-permute-start.1 = (bf16[2,384,2560]{1,2,0:T(8,128)(2,1)}, bf16[2,384,2560]{1,2,0:T(8,128)(2,1)}, u32[]{:S(2)}, u32[]{:S(2)}) collective-permute-start(bf16[2,384,2560]{1,2,0:T(8,128)(2,1)} %pad_maximum_fusion.9), channel_id=1, source_target_pairs={{8,0},{16,8},{24,16},{32,24},{40,32},{48,40},{56,48},{64,56},{72,6... | collective-permute-start | bytes 11796488 | tf_op jit(solution)/shard_map/ppermute | solution.py:21
  16.4 121.1 %collective-permute-start = (bf16[2,384,2560]{1,2,0:T(8,128)(2,1)}, bf16[2,384,2560]{1,2,0:T(8,128)(2,1)}, u32[]{:S(2)}, u32[]{:S(2)}) collective-permute-start(bf16[2,384,2560]{1,2,0:T(8,128)(2,1)} %pad_maximum_fusion.9), channel_id=1, source_target_pairs={{0,8},{8,16},{16,24},{24,32},{32,40},{40,48},{48,56},{56,64},{64,7... | collective-permute-start | bytes 11796488 | tf_op jit(solution)/shard_map/ppermute | solution.py:19
  33.0 0.7 copy-start.8
  33.1 1454.4 %all-gather.3.cloned.1.call-start = ((), (), s32[]{:S(2)}) async-start(), calls=%async_computation.1 | async-start | bytes 178257920 | tf_op jit(solution)/shard_map/all_gather | solution.py:145
  38.0 99.5 %copy-start.3 = (bf16[1,384,2560]{1,2,0:T(8,128)(2,1)S(1)}, bf16[1,384,2560]{1,2,0:T(8,128)(2,1)}, u32[]{:S(2)}) copy-start(bf16[1,384,2560]{1,2,0:T(8,128)(2,1)} %copy-done.2) | copy-start | bytes 5898244
  548.3 30.5 %copy-start.6 = (f32[384,20,128]{0,2,1:T(8,128)S(1)}, f32[384,20,128]{0,2,1:T(8,128)}, u32[]{:S(2)}) copy-start(f32[384,20,128]{0,2,1:T(8,128)} %get-tuple-element.181) | copy-start | bytes 11796484
  548.3 204.0 %slice-start.3 = ((s8[11796480]{0:T(1024)(128)(4,1)}), s8[4194304]{0:T(1024)(128)(4,1)S(1)}, s32[]{:S(2)}) async-start(s8[11796480]{0:T(1024)(128)(4,1)} %bitcast.167), calls=%async_computation.5 | async-start | bytes 8388608
  548.3 204.0 %slice-start.4 = ((s8[11796480]{0:T(1024)(128)(4,1)}), s8[4194304]{0:T(1024)(128)(4,1)S(1)}, s32[]{:S(2)}) async-start(s8[11796480]{0:T(1024)(128)(4,1)} %bitcast.167), calls=%async_computation.6 | async-start | bytes 8388608
  565.7 13.1 copy-start.4
  565.7 186.7 %slice-start = ((s8[11796480]{0:T(1024)(128)(4,1)}), s8[4194304]{0:T(1024)(128)(4,1)S(1)}, s32[]{:S(2)}) async-start(s8[11796480]{0:T(1024)(128)(4,1)} %bitcast.163), calls=%async_computation.2 | async-start | bytes 8388608
  565.7 186.7 %slice-start.1 = ((s8[11796480]{0:T(1024)(128)(4,1)}), s8[4194304]{0:T(1024)(128)(4,1)S(1)}, s32[]{:S(2)}) async-start(s8[11796480]{0:T(1024)(128)(4,1)} %bitcast.163), calls=%async_computation.3 | async-start | bytes 8388608
  565.7 186.7 %slice-start.5 = ((s8[11796480]{0:T(1024)(128)(4,1)}), s8[3407872]{0:T(1024)(128)(4,1)S(1)}, s32[]{:S(2)}) async-start(s8[11796480]{0:T(1024)(128)(4,1)} %bitcast.167), calls=%async_computation.7 | async-start | bytes 6815744
  572.5 174.2 %collective-permute-start.3 = (bf16[2,384,2560]{1,2,0:T(8,128)(2,1)}, bf16[2,384,2560]{1,2,0:T(8,128)(2,1)}, u32[]{:S(2)}, u32[]{:S(2)}) collective-permute-start(bf16[2,384,2560]{1,2,0:T(8,128)(2,1)} %get-tuple-element.191), channel_id=1, source_target_pairs={{0,8},{8,16},{16,24},{24,32},{32,40},{40,48},{48,56},{56,64},{64,7... | collective-permute-start | bytes 11796488 | tf_op jit(solution)/shard_map/ppermute | solution.py:36
  576.4 175.9 %collective-permute-start.2 = (bf16[2,384,2560]{1,2,0:T(8,128)(2,1)}, bf16[2,384,2560]{1,2,0:T(8,128)(2,1)}, u32[]{:S(2)}, u32[]{:S(2)}) collective-permute-start(bf16[2,384,2560]{1,2,0:T(8,128)(2,1)} %get-tuple-element.190), channel_id=1, source_target_pairs={{8,0},{16,8},{24,16},{32,24},{40,32},{48,40},{56,48},{64,56},{72,6... | collective-permute-start | bytes 11796488 | tf_op jit(solution)/shard_map/ppermute | solution.py:36
  578.8 173.6 %slice-start.2 = ((s8[11796480]{0:T(1024)(128)(4,1)}), s8[3407872]{0:T(1024)(128)(4,1)S(1)}, s32[]{:S(2)}) async-start(s8[11796480]{0:T(1024)(128)(4,1)} %bitcast.163), calls=%async_computation.4 | async-start | bytes 6815744
  756.4 2.1 copy-start.5
  761.5 6.1 collective-permute-start.4
  1549.5 7.9 copy-start.1
Sparse Core Ops, SparseCore 0:
  33.2 140.4 all-reduce.2
  522.0 965.4 all-gather.2
